TPU v7x, 32 devices: a whole 2x2x4 slice. The times are simulated.
32 devices in a mesh: groups: 2 (over y), req: 4 (over z), head: 2 (over x), sub: 2 (over core).
Axes of the slice: x: 2, y: 2, z: 4, core: 2. Of those that a mesh axis runs over, the one named last changes fastest.
Arguments:
- hidden_in: bfloat16 [1024, 8192], P(('groups', 'req')), parts along dimension 0, may hold values from -3 to 3
- q_weight: bfloat16 [8192, 8192], P('req', ('head', 'sub')), may hold values from -0.0625 to 0.0625
- q_gain: float32 [128], replicated, may hold values from 0.1 to 1.9
- key_cache: bfloat16 [8, 1601, 1024], P(('groups', 'req'), None, 'head'), parts along dimension 0, may hold values from -64 to 64
- value_cache: bfloat16 [8, 1601, 1024], P(('groups', 'req'), None, 'head'), parts along dimension 0, may hold values from -8 to 8
- out_weight: bfloat16 [8192, 8192], P(('head', 'sub'), 'req'), may hold values from -0.09375 to 0.09375
- req_image: int32 [1024], P(('groups', 'req')), parts along dimension 0, may hold values from 0 to 3, as said below
- image_count: int32 [1024], P(('groups', 'req')), parts along dimension 0, may hold values from 0 to 1, as said below
- image_home: int32 [8], P('groups'), parts along dimension 0, may hold values from 0 to 3, as said below
Outputs:
- layer_out: bfloat16 [1024, 8192], P(('groups', 'req'), ('head', 'sub')), parts along dimension 0
There are 2 independent parts, one for each index of `groups`. A program takes and returns all parts, laid end to end along the dimension named above; an argument that names none is the same for every part. Nothing has to cross between parts.
Inputs may be any that keep to these rules, and one draw needn't show every extreme that they name: Requests with image_count 0 attend to nothing; in each aligned block of 128 requests at most a quarter have image_count 0. In each aligned block of 128 requests, at most 64 requests with image_count 1 have one and the same value of image_home[req_image]; in every block exactly 64 of them share one value, and that value is the same for all blocks. `image_home`: each cache row holds exactly one image.
All inputs are finite; a program needn't handle non-finite values.
Results may differ from a plain program's by a relative error of at most 0.025.
Values may be sent and summed in bfloat16 or wider, within the bound.
A program may use at most 128 MiB of HBM per device.

v0:
```python
import jax
import jax.numpy as jnp
from jax import lax
from jax.sharding import PartitionSpec as P

HQ = 64
KVH = 8


def normalize_heads(queries, q_gain, head_dim):
    row_count = queries.shape[0]
    per_head = queries.astype(jnp.float32).reshape(row_count, -1, head_dim)
    inv_rms = lax.rsqrt(jnp.mean(per_head * per_head, axis=2, keepdims=True) + 1e-05)
    return (per_head * inv_rms * q_gain).reshape(row_count, -1).astype(jnp.bfloat16)


def local(
    hidden_in,
    q_weight,
    q_gain,
    key_cache,
    value_cache,
    out_weight,
    req_image,
    image_count,
    image_home,
):
    req_count = lax.axis_size("req")
    local_rows = hidden_in.shape[0]
    q_cols = q_weight.shape[1]
    head_dim = q_gain.shape[0]
    group_size = HQ // KVH
    heads_here = q_cols // head_dim
    spread_cols = lax.all_to_all(hidden_in, "req", split_axis=1, concat_axis=0, tiled=True)
    query_sum = lax.psum_scatter(
        jnp.dot(spread_cols, q_weight, preferred_element_type=jnp.float32).astype(jnp.bfloat16),
        "req",
        scatter_dimension=0,
        tiled=True,
    )
    queries = lax.optimization_barrier(query_sum)
    normalized = normalize_heads(queries, q_gain, head_dim)
    capacity = 2 * local_rows // req_count
    slot_total = req_count * capacity
    table_ids = lax.broadcasted_iota(jnp.int32, (local_rows, image_home.shape[0]), 1)
    home_rows = jnp.sum(jnp.where(req_image[:, None] == table_ids, image_home[None, :], 0), axis=1)
    wanted = image_count == 1
    dest_ids = lax.broadcasted_iota(jnp.int32, (local_rows, req_count), 1)
    to_dest = ((home_rows[:, None] == dest_ids) & wanted[:, None]).astype(jnp.int32)
    earlier = jnp.cumsum(to_dest, axis=0) - to_dest
    position = home_rows * capacity + jnp.sum(earlier * to_dest, axis=1)
    slot_ids = lax.broadcasted_iota(jnp.int32, (slot_total, local_rows), 0)
    dispatch = ((slot_ids == position[None, :]) & wanted[None, :]).astype(jnp.bfloat16)
    outgoing = jnp.dot(dispatch, normalized, preferred_element_type=jnp.float32).astype(
        jnp.bfloat16
    )
    outgoing = outgoing.reshape(req_count, capacity, q_cols)
    kv_count = max(1, heads_here // group_size)
    per_kv = heads_here // kv_count
    sub_index = lax.axis_index("sub")
    kv_first = sub_index * heads_here // group_size
    keys_here = lax.dynamic_slice_in_dim(
        key_cache[0], kv_first * head_dim, kv_count * head_dim, 1
    ).reshape(-1, kv_count, head_dim)
    values_here = lax.dynamic_slice_in_dim(
        value_cache[0], kv_first * head_dim, kv_count * head_dim, 1
    ).reshape(-1, kv_count, head_dim)
    score_scale = head_dim ** (-0.5)
    arrived = lax.all_to_all(outgoing, "req", split_axis=0, concat_axis=0, tiled=True)
    sources = arrived.shape[0]
    slot_count = arrived.shape[1]
    flat_rows = arrived.reshape(sources * slot_count, kv_count, per_kv, head_dim)
    scores = (
        jnp.einsum("mkgd,tkd->kgmt", flat_rows, keys_here, preferred_element_type=jnp.float32)
        * score_scale
    )
    row_peak = jnp.max(scores, axis=3, keepdims=True)
    weights = jnp.exp(scores - row_peak)
    probs = (weights / jnp.sum(weights, axis=3, keepdims=True)).astype(jnp.bfloat16)
    mixed_heads = jnp.einsum(
        "kgmt,tkd->mkgd", probs, values_here, preferred_element_type=jnp.float32
    )
    replies = mixed_heads.astype(jnp.bfloat16).reshape(sources, slot_count, q_cols)
    returned = lax.all_to_all(replies, "req", split_axis=0, concat_axis=0, tiled=True)
    attended = lax.dot_general(
        dispatch,
        returned.reshape(slot_total, q_cols),
        (((0,), (0,)), ((), ())),
        preferred_element_type=jnp.float32,
    ).astype(jnp.bfloat16)
    partial_cols = jnp.dot(
        lax.all_gather(attended, "req", axis=0, tiled=True),
        out_weight,
        preferred_element_type=jnp.float32,
    )
    head_terms = lax.all_to_all(
        partial_cols.astype(jnp.bfloat16), "req", split_axis=0, concat_axis=1, tiled=True
    )
    head_total = lax.psum_scatter(
        head_terms, ("head", "sub"), scatter_dimension=1, tiled=True
    ).astype(jnp.float32)
    out_width = head_total.shape[1]
    column_index = lax.axis_index("head") * lax.axis_size("sub") + lax.axis_index("sub")
    residual = lax.dynamic_slice_in_dim(hidden_in, column_index * out_width, out_width, 1)
    return (residual.astype(jnp.float32) + head_total).astype(jnp.bfloat16)


def solution(mesh):
    in_specs = (
        P(("groups", "req"), None),
        P("req", ("head", "sub")),
        P(),
        P(("groups", "req"), None, "head"),
        P(("groups", "req"), None, "head"),
        P(("head", "sub"), "req"),
        P(("groups", "req")),
        P(("groups", "req")),
        P("groups"),
    )
    out_specs = P(("groups", "req"), ("head", "sub"))
    return jax.shard_map(local, mesh=mesh, in_specs=in_specs, out_specs=out_specs, check_vma=False)
```

profile of v0, /device:TPU:0, one launch (start us, length us, event | category | flops | bytes accessed | tf_op | source)
XLA Modules:
  0.0 355.9 jit_solution(17557983354356708979)
XLA Ops:
  6.5 0.0 copy-start
  6.5 0.0 reduce-scatter.3.cloned.1.call-start
  6.5 4.1 %copy.39 = bf16[128,8192]{0,1:T(8,128)(2,1)} copy(bf16[128,8192]{1,0:T(8,128)(2,1)} %param.9) | data formatting | bytes 4194304 | tf_op args[0]
  10.6 54.5 %all_to_all.48 = bf16[128,4,2048]{0,2,1:T(8,128)(2,1)S(1)} all-to-all(bf16[128,4,2048]{0,2,1:T(8,128)(2,1)} %bitcast.58), channel_id=1, replica_groups=mesh['groups'=2,'req'=4,'head'=2,'sub'=2] {'req'}, dimensions={1} | all-to-all | bytes 4194304 | tf_op jit(solution)/shard_map/all_to_all | solution.py:34
  65.2 2.7 copy.40
  67.8 0.0 copy-start.3
  67.8 0.0 copy-start.4
  67.8 0.0 copy-start.5
  67.8 9.9 %convolution_convert_fusion.1 = bf16[512,2048]{1,0:T(8,128)(2,1)} fusion(bf16[512,2048]{1,0:T(8,128)(2,1)} %bitcast.63, bf16[2048,2048]{1,0:T(8,128)(2,1)} %param.10), kind=kOutput, calls=%fused_computation.11 | convolution fusion | flops 4296015872 | bytes 12582912 | tf_op jit(solution)/shard_map/dot_general | solution.py:36
  77.7 0.0 reduce-scatter.3.cloned.1.call-update
  77.8 0.0 copy-done.3
  77.8 0.0 copy-done.4
  77.8 0.2 select_reduce_fusion.1
  78.0 0.0 copy-done.5
  78.0 0.1 fusion.30
  78.1 0.2 reduce_window_sum.11
  78.3 0.2 select_reduce_fusion
  78.5 0.0 copy-done
  78.5 42.5 %reduce-scatter.3.cloned.1.call-done = bf16[128,2048]{1,0:T(8,128)(2,1)} async-done(((bf16[512,2048]{1,0:T(8,128)(2,1)}), bf16[128,2048]{1,0:T(8,128)(2,1)}) %reduce-scatter.3.cloned.1.call-update) | async-done | bytes 524304 | tf_op jit(solution)/shard_map/reduce_scatter | solution.py:35
  121.0 0.0 copy-start.2
  121.0 1.2 fusion.12
  122.2 0.2 copy.55
  122.4 0.3 reduce_sum.38
  122.8 0.1 copy.41
  122.8 0.1 copy.42
  123.0 0.3 mul.74
  123.3 0.0 copy-done.2
  123.3 1.6 convolution_convert_fusion.2
  124.9 3.5 all-to-all-start.1
  128.4 0.2 all-gather.2.cloned.1.call-start
  128.7 1.5 constant_dynamic-slice_fusion
  130.2 1.4 copy.38
  131.5 0.7 copy.37
  132.2 22.0 %all-to-all-done.1 = bf16[4,64,2048]{2,1,0:T(8,128)(2,1)S(1)} async-done(((bf16[4,64,2048]{2,1,0:T(8,128)(2,1)}), bf16[4,64,2048]{2,1,0:T(8,128)(2,1)S(1)}, u32[]{:S(2)}, u32[]{:S(2)}) %all-to-all-start.1) | async-done | bytes 1048608 | tf_op jit(solution)/shard_map/all_to_all | solution.py:69
  154.2 0.2 copy.57
  154.5 14.5 %fusion.34 = (f32[2,8,256]{2,1,0:T(8,128)S(1)}, f32[2,8,256,1601]{2,3,1,0:T(8,128)}) fusion(bf16[1601,2,128,1]{0,2,3,1:T(8,128)(2,1)} %bitcast.67, bf16[256,2,8,128]{3,2,1,0:T(8,128)(2,1)S(1)} %bitcast.65), kind=kOutput, calls=%fused_computation.45 | convolution fusion | flops 1698444800 | bytes 28115456 | tf_op jit(solution)/shard_map/sub | solution.py:78
  169.0 11.1 %fusion.11 = bf16[256,2,8,128]{0,3,2,1:T(8,128)(2,1)S(1)} fusion(bf16[1601,2,128,1]{0,2,3,1:T(8,128)(2,1)S(1)} %bitcast.66, f32[2,8,256,1601]{2,3,1,0:T(8,128)} %get-tuple-element.6, f32[2,8,256]{2,1,0:T(8,128)S(1)} %get-tuple-element.5), kind=kOutput, calls=%fused_computation.15 | convolution fusion | flops 1692409856 | bytes 28115456 | tf_op jit(solution)/shard_map/kgmt,tkd->mkgd/dot_general | solution.py:80
  180.1 1.1 copy.46
  181.2 0.5 reshape.59
  181.7 27.7 %all_to_all.49 = bf16[4,64,2048]{2,1,0:T(8,128)(2,1)S(1)} all-to-all(bf16[4,64,2048]{2,1,0:T(8,128)(2,1)S(1)} %reshape.59), channel_id=1, replica_groups=mesh['groups'=2,'req'=4,'head'=2,'sub'=2] {'req'}, dimensions={0} | all-to-all | bytes 2097152 | tf_op jit(solution)/shard_map/all_to_all | solution.py:84
  209.4 1.1 convolution_convert_fusion.3
  210.5 0.0 all-gather.2.cloned.1.call-update
  210.6 0.0 reduce-scatter.5.cloned.1.call-start
  210.6 45.0 %all-gather.2.cloned.1.call-done = bf16[512,2048]{1,0:T(8,128)(2,1)} async-done(((bf16[128,2048]{1,0:T(8,128)(2,1)}), bf16[512,2048]{1,0:T(8,128)(2,1)}) %all-gather.2.cloned.1.call-update) | async-done | bytes 2097168 | tf_op jit(solution)/shard_map/all_gather | solution.py:92
  255.7 8.5 %convolution_convert_fusion = bf16[512,2048]{1,0:T(8,128)(2,1)S(1)} fusion(bf16[512,2048]{1,0:T(8,128)(2,1)} %all-gather.2.cloned.1.call-done, bf16[2048,2048]{1,0:T(8,128)(2,1)} %param.14), kind=kOutput, calls=%fused_computation.10 | convolution fusion | flops 4296015872 | bytes 12582912 | tf_op jit(solution)/shard_map/dot_general | solution.py:91
  264.2 0.0 copy-start.1
  264.2 50.9 %all_to_all.50 = bf16[4,128,2048]{2,1,0:T(8,128)(2,1)S(1)} all-to-all(bf16[4,128,2048]{2,1,0:T(8,128)(2,1)S(1)} %bitcast.64), channel_id=1, replica_groups=mesh['groups'=2,'req'=4,'head'=2,'sub'=2] {'req'}, dimensions={0} | all-to-all | bytes 4194304 | tf_op jit(solution)/shard_map/all_to_all | solution.py:96
  315.1 1.5 copy.54
  316.6 0.0 reduce-scatter.5.cloned.1.call-update
  316.6 30.6 %reduce-scatter.5.cloned.1.call-done = bf16[128,2048]{1,0:T(8,128)(2,1)} async-done(((bf16[128,8192]{1,0:T(8,128)(2,1)}), bf16[128,2048]{1,0:T(8,128)(2,1)}) %reduce-scatter.5.cloned.1.call-update) | async-done | bytes 524304 | tf_op jit(solution)/shard_map/reduce_scatter | solution.py:99
  347.2 2.1 add_convert_fusion
  349.3 0.0 copy-done.1
  (4 shorter events, 0.0 us)
Async XLA Ops:
  6.5 71.9 %copy-start = (f32[128]{0:T(128)S(1)}, f32[128]{0:T(128)}, u32[]{:S(2)}) copy-start(f32[128]{0:T(128)} %param.11) | copy-start | bytes 1540
  6.5 114.5 %reduce-scatter.3.cloned.1.call-start = ((), (), s32[]{:S(2)}) async-start(), calls=%async_computation.6 | async-start | bytes 2621440 | tf_op jit(solution)/shard_map/reduce_scatter | solution.py:35
  67.8 9.9 %copy-start.3 = (s32[4]{0:T(128)S(1)}, s32[4]{0:T(128)}, u32[]{:S(2)}) copy-start(s32[4]{0:T(128)} %param.17) | copy-start | bytes 52
  67.8 9.9 %copy-start.4 = (s32[128]{0:T(128)S(1)}, s32[128]{0:T(128)}, u32[]{:S(2)}) copy-start(s32[128]{0:T(128)} %param.15) | copy-start | bytes 1540
  67.8 10.1 %copy-start.5 = (s32[128]{0:T(128)S(1)}, s32[128]{0:T(128)}, u32[]{:S(2)}) copy-start(s32[128]{0:T(128)} %param.16) | copy-start | bytes 1540
  121.0 2.3 copy-start.2
  124.9 29.3 %all-to-all-start.1 = ((bf16[4,64,2048]{2,1,0:T(8,128)(2,1)}), bf16[4,64,2048]{2,1,0:T(8,128)(2,1)S(1)}, u32[]{:S(2)}, u32[]{:S(2)}) async-start(bf16[4,64,2048]{2,1,0:T(8,128)(2,1)} %bitcast.8), calls=%async_computation.2 | async-start | bytes 2097152 | tf_op jit(solution)/shard_map/all_to_all | solution.py:69
  128.4 127.2 %all-gather.2.cloned.1.call-start = ((), (), s32[]{:S(2)}) async-start(), calls=%async_computation.7 | async-start | bytes 2621440 | tf_op jit(solution)/shard_map/all_gather | solution.py:92
  210.6 136.7 %reduce-scatter.5.cloned.1.call-start = ((), (), s32[]{:S(2)}) async-start(), calls=%async_computation.8 | async-start | bytes 2621440 | tf_op jit(solution)/shard_map/reduce_scatter | solution.py:99
  264.2 85.2 %copy-start.1 = (f32[128]{0:T(128)S(1)}, f32[128]{0:T(128)}, u32[]{:S(2)}) copy-start(f32[128]{0:T(128)} %param.11) | copy-start | bytes 1540
Sparse Core Ops, SparseCore 0:
  77.9 43.0 reduce-scatter.2
  210.7 44.9 all-gather.1
  316.8 30.4 reduce-scatter.4
where the time goes:
time: 356 us
  waiting for transfers between devices  140 us (39%)
  blocking collectives  133 us (37%)
  matrix products  46.8 us (13%)
  local copies, waits for them, and re-layouts  14.3 us (4%)
  between operations  13.3 us (4%)
  other arithmetic  4.32 us (1%)
  starting transfers between devices  3.78 us (1%)
    all_to_all x1, blocking collectives, local(): lax.all_to_all(hidden_in, 'req', split_axis=1, concat_axis=0, tiled=True)  54.5 us
    all_to_all x1, blocking collectives, local(): lax.all_to_all(partial_cols.astype(jnp.bfloat16), 'req', split_axis=0, co...  50.9 us
    all_gather x1, waiting for transfers between devices, local(): lax.all_gather(attended, 'req', axis=0, tiled=True)  45 us
    reduce_scatter x1, waiting for transfers between devices, local(): lax.psum_scatter(jnp.dot(spread_cols, q_weight, preferred_element_type=jn...  42.5 us
    reduce_scatter x1, waiting for transfers between devices, local(): lax.psum_scatter(head_terms, ('head', 'sub'), scatter_dimension=1, tiled=...  30.6 us
    all_to_all x1, blocking collectives, local(): lax.all_to_all(replies, 'req', split_axis=0, concat_axis=0, tiled=True)  27.7 us
    all_to_all x1, waiting for transfers between devices, local(): lax.all_to_all(outgoing, 'req', split_axis=0, concat_axis=0, tiled=True)  22 us
    sub x1, matrix products, local(): weights = jnp.exp(scores - row_peak)  14.5 us
  transfers between devices with their start and end apart: 4, of which 4 were waited for; matrix products, arithmetic and copies ran while one was open for 1% of the time, Pallas kernels for 0%

commit v1 on v0

--- a/solution.py
+++ b/solution.py
@@ -31,9 +31,25 @@
     head_dim = q_gain.shape[0]
     group_size = HQ // KVH
     heads_here = q_cols // head_dim
-    spread_cols = lax.all_to_all(hidden_in, "req", split_axis=1, concat_axis=0, tiled=True)
+    sub_count = lax.axis_size("sub")
+    part = q_weight.shape[0] // sub_count
+    mine = lax.dynamic_index_in_dim(
+        hidden_in.reshape(local_rows, req_count, sub_count, part),
+        lax.axis_index("sub"),
+        2,
+        keepdims=False,
+    )
+    mine = mine.transpose(1, 0, 2)
+    spread = lax.all_to_all(mine, "req", split_axis=0, concat_axis=0, tiled=True)
+    spread = lax.all_gather(spread.reshape(-1, part), "sub", axis=0, tiled=False)
+    query_part = jnp.einsum(
+        "kmi,kin->mn",
+        spread,
+        q_weight.reshape(sub_count, part, q_cols),
+        preferred_element_type=jnp.float32,
+    )
     query_sum = lax.psum_scatter(
-        jnp.dot(spread_cols, q_weight, preferred_element_type=jnp.float32).astype(jnp.bfloat16),
+        query_part.astype(jnp.bfloat16),
         "req",
         scatter_dimension=0,
         tiled=True,
@@ -93,12 +109,17 @@
         out_weight,
         preferred_element_type=jnp.float32,
     )
-    head_terms = lax.all_to_all(
-        partial_cols.astype(jnp.bfloat16), "req", split_axis=0, concat_axis=1, tiled=True
+    head_sum = lax.psum_scatter(
+        partial_cols.astype(jnp.bfloat16), ("head", "sub"), scatter_dimension=1, tiled=True
     )
-    head_total = lax.psum_scatter(
-        head_terms, ("head", "sub"), scatter_dimension=1, tiled=True
-    ).astype(jnp.float32)
+    piece = head_sum.shape[1]
+    by_owner = lax.all_to_all(
+        head_sum.reshape(req_count, local_rows, piece), "req", split_axis=0, concat_axis=0, tiled=True
+    )
+    lanes = lax.axis_size("head") * sub_count
+    blocks = lax.all_to_all(by_owner, ("head", "sub"), split_axis=0, concat_axis=0, tiled=True)
+    blocks = blocks.reshape(lanes, req_count // lanes, local_rows, piece)
+    head_total = blocks.transpose(2, 1, 0, 3).reshape(local_rows, -1).astype(jnp.float32)
     out_width = head_total.shape[1]
     column_index = lax.axis_index("head") * lax.axis_size("sub") + lax.axis_index("sub")
     residual = lax.dynamic_slice_in_dim(hidden_in, column_index * out_width, out_width, 1)

time: 356 us -> 327 us (0.919)
  blocking collectives: 133 us -> 78.8 us
  waiting for transfers between devices: 140 us -> 160 us
    all_to_all x2, blocking collectives: 105 us -> 51.1 us  [the longest x1 31.9 us: local(): lax.all_to_all(mine, 'req', split_axis=0, concat_axis=0, tiled=True)]
    all_gather x0 -> x1, waiting for transfers between devices: none -> 9.8 us  [local(): lax.all_gather(spread.reshape(-1, part), 'sub', axis=0, tiled=False)]
    all_to_all x0 -> x1, waiting for transfers between devices: none -> 8.79 us  [local(): lax.all_to_all(by_owner, ('head', 'sub'), split_axis=0, concat_axis=0, ti...]
    all_to_all x2 -> x0, local copies, waits for them, and re-layouts: 4.17 us -> none  [the longest x1 2.68 us: local(): lax.all_to_all(hidden_in, 'req', split_axis=1, concat_axis=0, tiled=True)]
    unnamed x15, local copies, waits for them, and re-layouts: 4.55 us -> 0.78 us
  transfers between devices with their start and end apart: 4 -> 6, of which waited for: 4 -> 6; matrix products, arithmetic and copies ran while one was open for 1% -> 1% of each run, Pallas kernels for 0% -> 0%
where the time goes in v1:
time: 327 us; the launch traced here: 326 us
  waiting for transfers between devices  160 us (49%)
  blocking collectives  78.8 us (24%)
  matrix products  48.1 us (15%)
  local copies, waits for them, and re-layouts  13.9 us (4%)
  between operations  13.4 us (4%)
  starting transfers between devices  7.29 us (2%)
  other arithmetic  4.29 us (1%)
    all_gather x1, waiting for transfers between devices, local(): lax.all_gather(attended, 'req', axis=0, tiled=True)  45 us
    reduce_scatter x1, waiting for transfers between devices, local(): lax.psum_scatter(query_part.astype(jnp.bfloat16), 'req', scatter_dimensio...  44.5 us
    all_to_all x1, blocking collectives, local(): lax.all_to_all(mine, 'req', split_axis=0, concat_axis=0, tiled=True)  31.9 us
    reduce_scatter x1, waiting for transfers between devices, local(): lax.psum_scatter(partial_cols.astype(jnp.bfloat16), ('head', 'sub'), scat...  30.3 us
    all_to_all x1, blocking collectives, local(): lax.all_to_all(replies, 'req', split_axis=0, concat_axis=0, tiled=True)  27.7 us
    all_to_all x1, waiting for transfers between devices, local(): lax.all_to_all(outgoing, 'req', split_axis=0, concat_axis=0, tiled=True)  22 us
    all_to_all x1, blocking collectives, local(): lax.all_to_all(head_sum.reshape(req_count, local_rows, piece), 'req', spl...  19.2 us
    sub x1, matrix products, local(): weights = jnp.exp(scores - row_peak)  14.5 us
  transfers between devices with their start and end apart: 6, of which 6 were waited for; matrix products, arithmetic and copies ran while one was open for 1% of the time, Pallas kernels for 0%

profile of v1, /device:TPU:0, one launch (start us, length us, event | category | flops | bytes accessed | tf_op | source)
XLA Modules:
  0.0 326.3 jit_solution(15593407834280450408)
XLA Ops:
  6.5 0.0 copy-start
  6.5 0.0 all-gather.3.cloned.1.call-start
  6.5 3.3 %reshape.66 = bf16[128,4,2,1024]{3,2,1,0:T(2,128)(2,1)S(1)} reshape(bf16[128,8192]{1,0:T(8,128)(2,1)} %param.9) | data formatting | bytes 4194304 | tf_op jit(solution)/shard_map/reshape | solution.py:37
  9.8 2.4 constant_dynamic-slice_fusion.2
  12.3 1.1 copy.72
  13.4 31.9 %all_to_all.25 = bf16[4,128,1024]{2,1,0:T(8,128)(2,1)} all-to-all(bf16[4,128,1024]{2,1,0:T(8,128)(2,1)S(1)} %bitcast.68), channel_id=1, replica_groups=mesh['groups'=2,'req'=4,'head'=2,'sub'=2] {'req'}, dimensions={0} | all-to-all | bytes 2097152 | tf_op jit(solution)/shard_map/all_to_all | solution.py:43
  45.4 0.0 all-gather.3.cloned.1.call-update
  45.4 0.0 reduce-scatter.3.cloned.1.call-start
  45.4 9.8 %all-gather.3.cloned.1.call-done = bf16[2,512,1024]{2,1,0:T(8,128)(2,1)} async-done(((bf16[1,512,1024]{2,1,0:T(8,128)(2,1)}), bf16[2,512,1024]{2,1,0:T(8,128)(2,1)}) %all-gather.3.cloned.1.call-update) | async-done | bytes 2097168 | tf_op jit(solution)/shard_map/all_gather | solution.py:44
  55.2 0.0 copy-start.3
  55.2 0.0 copy-start.4
  55.2 0.0 copy-start.5
  55.2 9.9 %bitcast_convert_fusion = bf16[512,2048]{1,0:T(8,128)(2,1)} fusion(bf16[2,512,1024]{2,1,0:T(8,128)(2,1)} %all-gather.3.cloned.1.call-done, bf16[2,1024,2048]{2,1,0:T(8,128)(2,1)} %bitcast.79), kind=kOutput, calls=%fused_computation.9 | convolution fusion | flops 4296015872 | bytes 12582912 | tf_op jit(solution)/shard_map/kmi,kin->mn/dot_general | solution.py:45
  65.1 0.0 reduce-scatter.3.cloned.1.call-update
  65.1 0.0 copy-done.3
  65.1 0.0 copy-done.4
  65.1 0.2 select_reduce_fusion.1
  65.3 0.0 copy-done.5
  65.3 0.1 fusion.30
  65.4 0.2 reduce_window_sum.11
  65.6 0.2 select_reduce_fusion
  65.8 0.0 copy-done
  65.8 44.5 %reduce-scatter.3.cloned.1.call-done = bf16[128,2048]{1,0:T(8,128)(2,1)} async-done(((bf16[512,2048]{1,0:T(8,128)(2,1)}), bf16[128,2048]{1,0:T(8,128)(2,1)}) %reduce-scatter.3.cloned.1.call-update) | async-done | bytes 524304 | tf_op jit(solution)/shard_map/reduce_scatter | solution.py:51
  110.3 0.0 copy-start.2
  110.3 1.2 fusion.12
  111.5 0.2 copy.53
  111.7 0.3 reduce_sum.38
  112.1 0.1 copy.40
  112.1 0.1 copy.41
  112.3 0.3 mul.74
  112.6 0.0 copy-done.2
  112.6 1.6 convolution_convert_fusion.1
  114.2 3.5 %all-to-all-start.1 = ((bf16[4,64,2048]{2,1,0:T(8,128)(2,1)}), bf16[4,64,2048]{2,1,0:T(8,128)(2,1)S(1)}, u32[]{:S(2)}, u32[]{:S(2)}) async-start(bf16[4,64,2048]{2,1,0:T(8,128)(2,1)} %bitcast.10), calls=%async_computation.2 | async-start | bytes 2097152 | tf_op jit(solution)/shard_map/all_to_all | solution.py:85
  117.7 0.2 all-gather.5.cloned.1.call-start
  118.0 1.5 constant_dynamic-slice_fusion
  119.5 1.3 copy.38
  120.8 0.7 copy.37
  121.5 22.0 %all-to-all-done.1 = bf16[4,64,2048]{2,1,0:T(8,128)(2,1)S(1)} async-done(((bf16[4,64,2048]{2,1,0:T(8,128)(2,1)}), bf16[4,64,2048]{2,1,0:T(8,128)(2,1)S(1)}, u32[]{:S(2)}, u32[]{:S(2)}) %all-to-all-start.1) | async-done | bytes 1048608 | tf_op jit(solution)/shard_map/all_to_all | solution.py:85
  143.5 0.2 copy.55
  143.8 14.5 %fusion.34 = (f32[2,8,256]{2,1,0:T(8,128)S(1)}, f32[2,8,256,1601]{2,3,1,0:T(8,128)}) fusion(bf16[1601,2,128,1]{0,2,3,1:T(8,128)(2,1)} %bitcast.77, bf16[256,2,8,128]{3,2,1,0:T(8,128)(2,1)S(1)} %bitcast.75), kind=kOutput, calls=%fused_computation.48 | convolution fusion | flops 1698444800 | bytes 28115456 | tf_op jit(solution)/shard_map/sub | solution.py:94
  158.3 11.1 %fusion.11 = bf16[256,2,8,128]{0,3,2,1:T(8,128)(2,1)S(1)} fusion(bf16[1601,2,128,1]{0,2,3,1:T(8,128)(2,1)S(1)} %bitcast.76, f32[2,8,256,1601]{2,3,1,0:T(8,128)} %get-tuple-element.6, f32[2,8,256]{2,1,0:T(8,128)S(1)} %get-tuple-element.5), kind=kOutput, calls=%fused_computation.15 | convolution fusion | flops 1692409856 | bytes 28115456 | tf_op jit(solution)/shard_map/kgmt,tkd->mkgd/dot_general | solution.py:96
  169.4 1.1 copy.45
  170.5 0.5 reshape.70
  171.0 27.7 %all_to_all.26 = bf16[4,64,2048]{2,1,0:T(8,128)(2,1)S(1)} all-to-all(bf16[4,64,2048]{2,1,0:T(8,128)(2,1)S(1)} %reshape.70), channel_id=1, replica_groups=mesh['groups'=2,'req'=4,'head'=2,'sub'=2] {'req'}, dimensions={0} | all-to-all | bytes 2097152 | tf_op jit(solution)/shard_map/all_to_all | solution.py:100
  198.7 1.1 convolution_convert_fusion.2
  199.8 0.0 all-gather.5.cloned.1.call-update
  199.9 0.0 reduce-scatter.5.cloned.1.call-start
  199.9 45.0 %all-gather.5.cloned.1.call-done = bf16[512,2048]{1,0:T(8,128)(2,1)} async-done(((bf16[128,2048]{1,0:T(8,128)(2,1)}), bf16[512,2048]{1,0:T(8,128)(2,1)}) %all-gather.5.cloned.1.call-update) | async-done | bytes 2097168 | tf_op jit(solution)/shard_map/all_gather | solution.py:108
  244.9 9.9 %convolution_convert_fusion = bf16[512,2048]{1,0:T(8,128)(2,1)} fusion(bf16[512,2048]{1,0:T(8,128)(2,1)} %all-gather.5.cloned.1.call-done, bf16[2048,2048]{1,0:T(8,128)(2,1)} %param.14), kind=kOutput, calls=%fused_computation.11 | convolution fusion | flops 4296015872 | bytes 12582912 | tf_op jit(solution)/shard_map/dot_general | solution.py:107
  254.8 0.0 reduce-scatter.5.cloned.1.call-update
  254.8 30.3 %reduce-scatter.5.cloned.1.call-done = bf16[512,512]{1,0:T(8,128)(2,1)} async-done(((bf16[512,2048]{1,0:T(8,128)(2,1)}), bf16[512,512]{1,0:T(8,128)(2,1)}) %reduce-scatter.5.cloned.1.call-update) | async-done | bytes 524304 | tf_op jit(solution)/shard_map/reduce_scatter | solution.py:112
  285.1 19.2 %all_to_all.27 = bf16[4,128,512]{2,1,0:T(8,128)(2,1)} all-to-all(bf16[4,128,512]{2,1,0:T(8,128)(2,1)} %bitcast.78), channel_id=1, replica_groups=mesh['groups'=2,'req'=4,'head'=2,'sub'=2] {'req'}, dimensions={0} | all-to-all | bytes 1048576 | tf_op jit(solution)/shard_map/all_to_all | solution.py:116
  304.3 3.5 %all-to-all-start.4 = ((bf16[4,128,512]{2,1,0:T(8,128)(2,1)}), bf16[4,128,512]{2,1,0:T(8,128)(2,1)S(1)}, u32[]{:S(2)}, u32[]{:S(2)}) async-start(bf16[4,128,512]{2,1,0:T(8,128)(2,1)} %all_to_all.27), calls=%async_computation.6 | async-start | bytes 1048576 | tf_op jit(solution)/shard_map/all_to_all | solution.py:120
  307.8 0.0 copy-start.1
  307.8 8.8 %all-to-all-done.4 = bf16[4,128,512]{2,1,0:T(8,128)(2,1)S(1)} async-done(((bf16[4,128,512]{2,1,0:T(8,128)(2,1)}), bf16[4,128,512]{2,1,0:T(8,128)(2,1)S(1)}, u32[]{:S(2)}, u32[]{:S(2)}) %all-to-all-start.4) | async-done | bytes 524320 | tf_op jit(solution)/shard_map/all_to_all | solution.py:120
  316.6 0.1 convert_bitcast_fusion
  316.7 0.7 copy.46
  317.4 0.3 copy.56
  317.8 2.0 add_convert_fusion
  319.7 0.0 copy-done.1
  (4 shorter events, 0.0 us)
Async XLA Ops:
  6.5 59.3 %copy-start = (f32[128]{0:T(128)S(1)}, f32[128]{0:T(128)}, u32[]{:S(2)}) copy-start(f32[128]{0:T(128)} %param.11) | copy-start | bytes 1540
  6.5 48.7 %all-gather.3.cloned.1.call-start = ((), (), s32[]{:S(2)}) async-start(), calls=%async_computation.7 | async-start | bytes 3145728 | tf_op jit(solution)/shard_map/all_gather | solution.py:44
  45.4 64.9 %reduce-scatter.3.cloned.1.call-start = ((), (), s32[]{:S(2)}) async-start(), calls=%async_computation.8 | async-start | bytes 2621440 | tf_op jit(solution)/shard_map/reduce_scatter | solution.py:51
  55.2 9.9 %copy-start.3 = (s32[4]{0:T(128)S(1)}, s32[4]{0:T(128)}, u32[]{:S(2)}) copy-start(s32[4]{0:T(128)} %param.17) | copy-start | bytes 52
  55.2 9.9 %copy-start.4 = (s32[128]{0:T(128)S(1)}, s32[128]{0:T(128)}, u32[]{:S(2)}) copy-start(s32[128]{0:T(128)} %param.15) | copy-start | bytes 1540
  55.2 10.1 %copy-start.5 = (s32[128]{0:T(128)S(1)}, s32[128]{0:T(128)}, u32[]{:S(2)}) copy-start(s32[128]{0:T(128)} %param.16) | copy-start | bytes 1540
  110.3 2.3 copy-start.2
  114.2 29.3 %all-to-all-start.1 = ((bf16[4,64,2048]{2,1,0:T(8,128)(2,1)}), bf16[4,64,2048]{2,1,0:T(8,128)(2,1)S(1)}, u32[]{:S(2)}, u32[]{:S(2)}) async-start(bf16[4,64,2048]{2,1,0:T(8,128)(2,1)} %bitcast.10), calls=%async_computation.2 | async-start | bytes 2097152 | tf_op jit(solution)/shard_map/all_to_all | solution.py:85
  117.7 127.2 %all-gather.5.cloned.1.call-start = ((), (), s32[]{:S(2)}) async-start(), calls=%async_computation.9 | async-start | bytes 2621440 | tf_op jit(solution)/shard_map/all_gather | solution.py:108
  199.9 85.3 %reduce-scatter.5.cloned.1.call-start = ((), (), s32[]{:S(2)}) async-start(), calls=%async_computation.10 | async-start | bytes 2621440 | tf_op jit(solution)/shard_map/reduce_scatter | solution.py:112
  304.3 12.3 %all-to-all-start.4 = ((bf16[4,128,512]{2,1,0:T(8,128)(2,1)}), bf16[4,128,512]{2,1,0:T(8,128)(2,1)S(1)}, u32[]{:S(2)}, u32[]{:S(2)}) async-start(bf16[4,128,512]{2,1,0:T(8,128)(2,1)} %all_to_all.27), calls=%async_computation.6 | async-start | bytes 1048576 | tf_op jit(solution)/shard_map/all_to_all | solution.py:120
  307.8 11.9 %copy-start.1 = (f32[128]{0:T(128)S(1)}, f32[128]{0:T(128)}, u32[]{:S(2)}) copy-start(f32[128]{0:T(128)} %param.11) | copy-start | bytes 1540
Sparse Core Ops, SparseCore 0:
  45.5 9.6 all-gather.2
  65.2 45.0 reduce-scatter.2
  200.0 44.9 all-gather.4
  254.9 30.1 reduce-scatter.4

commit v2 on v1

--- a/solution.py
+++ b/solution.py
@@ -1,6 +1,10 @@
+import functools
+
 import jax
 import jax.numpy as jnp
 from jax import lax
+from jax.experimental import pallas as pl
+from jax.experimental.pallas import tpu as pltpu
 from jax.sharding import PartitionSpec as P
 
 HQ = 64
@@ -12,6 +16,214 @@
     per_head = queries.astype(jnp.float32).reshape(row_count, -1, head_dim)
     inv_rms = lax.rsqrt(jnp.mean(per_head * per_head, axis=2, keepdims=True) + 1e-05)
     return (per_head * inv_rms * q_gain).reshape(row_count, -1).astype(jnp.bfloat16)
+
+
+MESH = pl.DeviceIdType.MESH
+
+
+def out_kernel(
+    n,
+    lanes,
+    n_sub,
+    tile,
+    att_ref,
+    w_hbm,
+    res_ref,
+    out_ref,
+    w_v,
+    gath,
+    part,
+    rs,
+    fin,
+    land,
+    w_sem,
+    r_send,
+    l_send,
+    g_recv,
+    rs_send,
+    rs_recv,
+    f_send,
+    f_recv,
+):
+    g, r = lax.axis_index("groups"), lax.axis_index("req")
+    me = lax.axis_index("head") * n_sub + lax.axis_index("sub")
+    rows = att_ref.shape[0] // lanes
+    has_left, has_right = r > 0, r < n - 1
+    on_self = r == me
+
+    def dev(row, lane):
+        return (g, row, lax.div(lane, n_sub), lax.rem(lane, n_sub))
+
+    load = pltpu.make_async_copy(w_hbm, w_v, w_sem)
+    load.start()
+
+    barrier = pltpu.get_barrier_semaphore()
+
+    def greet(row, lane):
+        pl.semaphore_signal(barrier, inc=1, device_id=dev(row, lane), device_id_type=MESH)
+
+    pl.when(has_left)(lambda: greet(r - 1, me))
+    pl.when(has_right)(lambda: greet(r + 1, me))
+    for d in range(1, lanes):
+        greet(r, lax.rem(me + d, lanes))
+    for q in range(lanes):
+        pl.when(jnp.logical_not(on_self & (me == q)))(functools.partial(greet, me, jnp.int32(q)))
+    neighbours = jnp.where(has_left, 1, 0) + jnp.where(has_right, 1, 0)
+    pl.semaphore_wait(barrier, neighbours + (lanes - 1) + n - jnp.where(on_self, 1, 0))
+
+    def block_copy(src, ref, to_right):
+        return pltpu.make_async_remote_copy(
+            src_ref=ref,
+            dst_ref=gath.at[src],
+            send_sem=(r_send if to_right else l_send).at[src],
+            recv_sem=g_recv.at[src],
+            device_id=dev(r + 1 if to_right else r - 1, me),
+            device_id_type=MESH,
+        )
+
+    def part_copy(src, d):
+        lane = lax.rem(me + d, lanes)
+        return pltpu.make_async_remote_copy(
+            src_ref=part.at[src, lane],
+            dst_ref=rs.at[src, d],
+            send_sem=rs_send.at[src, d],
+            recv_sem=rs_recv.at[src, d],
+            device_id=dev(r, lane),
+            device_id_type=MESH,
+        )
+
+    def owner_copy(src):
+        return pltpu.make_async_remote_copy(
+            src_ref=fin.at[src],
+            dst_ref=land.at[me],
+            send_sem=f_send.at[src],
+            recv_sem=f_recv.at[me],
+            device_id=dev(src, r),
+            device_id_type=MESH,
+        )
+
+    def process(src, ref):
+        @pl.loop(0, w_v.shape[1] // tile)
+        def _(c):
+            cols = pl.ds(pl.multiple_of(c * tile, tile), tile)
+            product = jnp.dot(ref[...], w_v[:, cols], preferred_element_type=jnp.float32)
+            part[src, :, :, cols] = product.astype(jnp.bfloat16).reshape(lanes, rows, tile)
+
+        for d in range(1, lanes):
+            part_copy(src, d).start()
+
+    def finish(src):
+        total = part[src, me].astype(jnp.float32)
+        for d in range(1, lanes):
+            part_copy(src, d).wait_recv()
+            total += rs[src, d].astype(jnp.float32)
+        fin[src] = total.astype(jnp.bfloat16)
+        local_owner = on_self & (src == r)
+
+        @pl.when(local_owner)
+        def _():
+            land[me] = fin[src]
+
+        @pl.when(jnp.logical_not(local_owner))
+        def _():
+            owner_copy(src).start()
+
+    def finish_step(k):
+        if k == 0:
+            finish(r)
+        else:
+            pl.when(r >= k)(lambda: finish(r - k))
+            pl.when(r + k < n)(lambda: finish(r + k))
+
+    pl.when(has_right)(lambda: block_copy(r, att_ref, True).start())
+    pl.when(has_left)(lambda: block_copy(r, att_ref, False).start())
+    load.wait()
+    process(r, att_ref)
+    for k in range(1, n):
+
+        @pl.when(r >= k)
+        def _():
+            src = r - k
+            block_copy(src, gath.at[src], False).wait_recv()
+            pl.when(has_right)(lambda: block_copy(src, gath.at[src], True).start())
+            process(src, gath.at[src])
+
+        @pl.when(r + k < n)
+        def _():
+            src = r + k
+            block_copy(src, gath.at[src], True).wait_recv()
+            pl.when(has_left)(lambda: block_copy(src, gath.at[src], False).start())
+            process(src, gath.at[src])
+
+        finish_step(k - 1)
+    finish_step(n - 1)
+
+    for q in range(lanes):
+
+        @pl.when(jnp.logical_not(on_self & (me == q)))
+        def _():
+            pltpu.make_async_remote_copy(
+                src_ref=fin.at[0],
+                dst_ref=land.at[q],
+                send_sem=f_send.at[0],
+                recv_sem=f_recv.at[q],
+                device_id=dev(me, jnp.int32(q)),
+                device_id_type=MESH,
+            ).wait_recv()
+
+        here = pl.ds(q * rows, rows)
+        out_ref[here, :] = (
+            res_ref[here, :].astype(jnp.float32) + land[q].astype(jnp.float32)
+        ).astype(jnp.bfloat16)
+
+    pl.when(has_right)(lambda: block_copy(r, att_ref, True).wait_send())
+    pl.when(has_left)(lambda: block_copy(r, att_ref, False).wait_send())
+    for k in range(1, n):
+        pl.when((r >= k) & has_right)(
+            lambda: block_copy(r - k, gath.at[r - k], True).wait_send()
+        )
+        pl.when((r + k < n) & has_left)(
+            lambda: block_copy(r + k, gath.at[r + k], False).wait_send()
+        )
+    for src in range(n):
+        for d in range(1, lanes):
+            part_copy(src, d).wait_send()
+        pl.when(jnp.logical_not(on_self & (r == src)))(
+            lambda: owner_copy(jnp.int32(src)).wait_send()
+        )
+
+
+def project_out(attended, out_weight, residual, n, lanes, n_sub):
+    local_rows, depth = attended.shape
+    width = out_weight.shape[1]
+    rows = local_rows // lanes
+    vmem = pl.BlockSpec(memory_space=pltpu.VMEM)
+    dma = pltpu.SemaphoreType.DMA
+    return pl.pallas_call(
+        functools.partial(out_kernel, n, lanes, n_sub, min(width, 512)),
+        out_shape=jax.ShapeDtypeStruct((local_rows, width), jnp.bfloat16),
+        in_specs=[vmem, pl.BlockSpec(memory_space=pl.ANY), vmem],
+        out_specs=vmem,
+        scratch_shapes=[
+            pltpu.VMEM((depth, width), jnp.bfloat16),
+            pltpu.VMEM((n, local_rows, depth), jnp.bfloat16),
+            pltpu.VMEM((n, lanes, rows, width), jnp.bfloat16),
+            pltpu.VMEM((n, lanes, rows, width), jnp.bfloat16),
+            pltpu.VMEM((n, rows, width), jnp.bfloat16),
+            pltpu.VMEM((lanes, rows, width), jnp.bfloat16),
+            dma,
+            dma((n,)),
+            dma((n,)),
+            dma((n,)),
+            dma((n, lanes)),
+            dma((n, lanes)),
+            dma((n,)),
+            dma((lanes,)),
+        ],
+        compiler_params=pltpu.CompilerParams(
+            collective_id=0, has_side_effects=True, vmem_limit_bytes=40 * 1024 * 1024
+        ),
+    )(attended, out_weight, residual)
 
 
 def local(
@@ -104,6 +316,12 @@
         (((0,), (0,)), ((), ())),
         preferred_element_type=jnp.float32,
     ).astype(jnp.bfloat16)
+    lanes = lax.axis_size("head") * sub_count
+    column_index = lax.axis_index("head") * sub_count + lax.axis_index("sub")
+    if req_count == lanes and local_rows % (16 * lanes) == 0:
+        width = out_weight.shape[1]
+        residual = lax.dynamic_slice_in_dim(hidden_in, column_index * width, width, 1)
+        return project_out(attended, out_weight, residual, req_count, lanes, sub_count)
     partial_cols = jnp.dot(
         lax.all_gather(attended, "req", axis=0, tiled=True),
         out_weight,
@@ -116,12 +334,10 @@
     by_owner = lax.all_to_all(
         head_sum.reshape(req_count, local_rows, piece), "req", split_axis=0, concat_axis=0, tiled=True
     )
-    lanes = lax.axis_size("head") * sub_count
     blocks = lax.all_to_all(by_owner, ("head", "sub"), split_axis=0, concat_axis=0, tiled=True)
     blocks = blocks.reshape(lanes, req_count // lanes, local_rows, piece)
     head_total = blocks.transpose(2, 1, 0, 3).reshape(local_rows, -1).astype(jnp.float32)
     out_width = head_total.shape[1]
-    column_index = lax.axis_index("head") * lax.axis_size("sub") + lax.axis_index("sub")
     residual = lax.dynamic_slice_in_dim(hidden_in, column_index * out_width, out_width, 1)
     return (residual.astype(jnp.float32) + head_total).astype(jnp.bfloat16)
 

time: 327 us -> 270 us (0.83)
  waiting for transfers between devices: 160 us -> 101 us
  Pallas kernels: 0 us -> 55.9 us
  blocking collectives: 78.8 us -> 31.9 us
  matrix products: 48.1 us -> 38.5 us
  local copies, waits for them, and re-layouts: 13.9 us -> 19 us
    pallas_call x0 -> x1, Pallas kernels: none -> 55.9 us  [project_out(): pl.pallas_call(functools.partial(out_kernel, n, lanes, n_sub, min(width,...]
    all_to_all x2 -> x0, blocking collectives: 46.9 us -> none  [the longest x1 27.7 us: local(): lax.all_to_all(replies, 'req', split_axis=0, concat_axis=0, tiled=True)]
    all_gather x1 -> x0, waiting for transfers between devices: 45 us -> none  [local(): lax.all_gather(attended, 'req', axis=0, tiled=True)]
    reduce_scatter x1 -> x0, waiting for transfers between devices: 30.3 us -> none  [local(): lax.psum_scatter(partial_cols.astype(jnp.bfloat16), ('head', 'sub'), scat...]
    all_to_all x1, waiting for transfers between devices: 8.79 us -> 24.1 us  [local(): lax.all_to_all(replies, 'req', split_axis=0, concat_axis=0, tiled=True)]
    dot_general x1 -> x0, matrix products: 9.86 us -> none  [local(): jnp.dot(lax.all_gather(attended, 'req', axis=0, tiled=True), out_weight,...]
    unnamed x15, local copies, waits for them, and re-layouts: 0.78 us -> 4.61 us
  transfers between devices with their start and end apart: 6 -> 4, of which waited for: 6 -> 4; matrix products, arithmetic and copies ran while one was open for 1% -> 2% of each run, Pallas kernels for 0% -> 0%
where the time goes in v2:
time: 270 us; the launch traced here: 269 us
  waiting for transfers between devices  101 us (37%)
  Pallas kernels  55.9 us (21%)
  matrix products  38.5 us (14%)
  blocking collectives  31.9 us (12%)
  local copies, waits for them, and re-layouts  19 us (7%)
  between operations  13.6 us (5%)
  starting transfers between devices  7.25 us (3%)
    pallas_call x1, Pallas kernels, project_out(): pl.pallas_call(functools.partial(out_kernel, n, lanes, n_sub, min(width,...  55.9 us
    reduce_scatter x1, waiting for transfers between devices, local(): lax.psum_scatter(query_part.astype(jnp.bfloat16), 'req', scatter_dimensio...  44.5 us
    all_to_all x1, blocking collectives, local(): lax.all_to_all(mine, 'req', split_axis=0, concat_axis=0, tiled=True)  31.9 us
    all_to_all x1, waiting for transfers between devices, local(): lax.all_to_all(replies, 'req', split_axis=0, concat_axis=0, tiled=True)  24.1 us
    all_to_all x1, waiting for transfers between devices, local(): lax.all_to_all(outgoing, 'req', split_axis=0, concat_axis=0, tiled=True)  22.1 us
    sub x1, matrix products, local(): weights = jnp.exp(scores - row_peak)  14.5 us
    dot_general x1, matrix products, local(): jnp.einsum('kgmt,tkd->mkgd', probs, values_here, preferred_element_type=j...  11.1 us
    dot_general x1, matrix products, local(): jnp.einsum('kmi,kin->mn', spread, q_weight.reshape(sub_count, part, q_col...  9.84 us
  transfers between devices with their start and end apart: 4, of which 4 were waited for; matrix products, arithmetic and copies ran while one was open for 2% of the time, Pallas kernels for 0%

profile of v2, /device:TPU:0, one launch (start us, length us, event | category | flops | bytes accessed | tf_op | source)
XLA Modules:
  0.0 268.8 jit_solution(10981066097537956740)
XLA Ops:
  6.5 0.0 copy-start
  6.5 0.0 all-gather.2.cloned.1.call-start
  6.5 3.3 %reshape.57 = bf16[128,4,2,1024]{3,2,1,0:T(2,128)(2,1)S(1)} reshape(bf16[128,8192]{1,0:T(8,128)(2,1)} %param.9) | data formatting | bytes 4194304 | tf_op jit(solution)/shard_map/reshape | solution.py:249
  9.8 2.4 constant_dynamic-slice_fusion
  12.3 1.1 copy.66
  13.4 31.9 %all_to_all.15 = bf16[4,128,1024]{2,1,0:T(8,128)(2,1)} all-to-all(bf16[4,128,1024]{2,1,0:T(8,128)(2,1)S(1)} %bitcast.56), channel_id=1, replica_groups=mesh['groups'=2,'req'=4,'head'=2,'sub'=2] {'req'}, dimensions={0} | all-to-all | bytes 2097152 | tf_op jit(solution)/shard_map/all_to_all | solution.py:255
  45.4 0.0 all-gather.2.cloned.1.call-update
  45.4 0.0 reduce-scatter.2.cloned.1.call-start
  45.4 9.8 %all-gather.2.cloned.1.call-done = bf16[2,512,1024]{2,1,0:T(8,128)(2,1)} async-done(((bf16[1,512,1024]{2,1,0:T(8,128)(2,1)}), bf16[2,512,1024]{2,1,0:T(8,128)(2,1)}) %all-gather.2.cloned.1.call-update) | async-done | bytes 2097168 | tf_op jit(solution)/shard_map/all_gather | solution.py:256
  55.2 0.0 copy-start.3
  55.2 0.0 copy-start.4
  55.2 0.0 copy-start.5
  55.2 9.8 %bitcast_convert_fusion = bf16[512,2048]{1,0:T(8,128)(2,1)} fusion(bf16[2,512,1024]{2,1,0:T(8,128)(2,1)} %all-gather.2.cloned.1.call-done, bf16[2,1024,2048]{2,1,0:T(8,128)(2,1)} %bitcast.64), kind=kOutput, calls=%fused_computation.9 | convolution fusion | flops 4296015872 | bytes 12582912 | tf_op jit(solution)/shard_map/kmi,kin->mn/dot_general | solution.py:257
  65.1 0.0 reduce-scatter.2.cloned.1.call-update
  65.1 0.0 copy-done.3
  65.1 0.0 copy-done.4
  65.1 0.2 select_reduce_fusion.1
  65.3 0.0 copy-done.5
  65.3 0.1 fusion.30
  65.4 0.2 reduce_window_sum.11
  65.6 0.2 select_reduce_fusion
  65.8 0.0 copy-done
  65.8 44.5 %reduce-scatter.2.cloned.1.call-done = bf16[128,2048]{1,0:T(8,128)(2,1)} async-done(((bf16[512,2048]{1,0:T(8,128)(2,1)}), bf16[128,2048]{1,0:T(8,128)(2,1)}) %reduce-scatter.2.cloned.1.call-update) | async-done | bytes 524304 | tf_op jit(solution)/shard_map/reduce_scatter | solution.py:263
  110.3 1.1 fusion.12
  111.4 0.2 copy.48
  111.6 0.3 reduce_sum.38
  112.0 0.1 copy.36
  112.0 0.1 copy.37
  112.2 0.3 mul.72
  112.5 2.6 convolution_convert_fusion
  115.2 3.7 %all-to-all-start.1 = ((bf16[4,64,2048]{2,1,0:T(8,128)(2,1)}), bf16[4,64,2048]{2,1,0:T(8,128)(2,1)S(1)}, u32[]{:S(2)}, u32[]{:S(2)}) async-start(bf16[4,64,2048]{2,1,0:T(8,128)(2,1)} %bitcast.10), calls=%async_computation.2 | async-start | bytes 2097152 | tf_op jit(solution)/shard_map/all_to_all | solution.py:297
  118.9 1.5 constant_dynamic-slice_fusion.1
  120.4 1.4 copy.34
  121.8 0.7 copy.33
  122.4 22.1 %all-to-all-done.1 = bf16[4,64,2048]{2,1,0:T(8,128)(2,1)S(1)} async-done(((bf16[4,64,2048]{2,1,0:T(8,128)(2,1)}), bf16[4,64,2048]{2,1,0:T(8,128)(2,1)S(1)}, u32[]{:S(2)}, u32[]{:S(2)}) %all-to-all-start.1) | async-done | bytes 1048608 | tf_op jit(solution)/shard_map/all_to_all | solution.py:297
  144.5 0.2 copy.50
  144.7 14.5 %fusion.34 = (f32[2,8,256]{2,1,0:T(8,128)S(1)}, f32[2,8,256,1601]{2,3,1,0:T(8,128)}) fusion(bf16[1601,2,128,1]{0,2,3,1:T(8,128)(2,1)} %bitcast.63, bf16[256,2,8,128]{3,2,1,0:T(8,128)(2,1)S(1)} %bitcast.61), kind=kOutput, calls=%fused_computation.46 | convolution fusion | flops 1698444800 | bytes 28115456 | tf_op jit(solution)/shard_map/sub | solution.py:306
  159.3 11.1 %fusion.11 = bf16[256,2,8,128]{0,3,2,1:T(8,128)(2,1)S(1)} fusion(bf16[1601,2,128,1]{0,2,3,1:T(8,128)(2,1)S(1)} %bitcast.62, f32[2,8,256,1601]{2,3,1,0:T(8,128)} %get-tuple-element.6, f32[2,8,256]{2,1,0:T(8,128)S(1)} %get-tuple-element.5), kind=kOutput, calls=%fused_computation.14 | convolution fusion | flops 1692409856 | bytes 28115456 | tf_op jit(solution)/shard_map/kgmt,tkd->mkgd/dot_general | solution.py:308
  170.4 1.1 copy.41
  171.4 0.0 copy-start.1
  171.5 1.3 reshape.61
  172.8 3.5 %all-to-all-start.2 = ((bf16[4,64,2048]{2,1,0:T(8,128)(2,1)}), bf16[4,64,2048]{2,1,0:T(8,128)(2,1)S(1)}, u32[]{:S(2)}, u32[]{:S(2)}) async-start(bf16[4,64,2048]{2,1,0:T(8,128)(2,1)} %reshape.61), calls=%async_computation.3 | async-start | bytes 2097152 | tf_op jit(solution)/shard_map/all_to_all | solution.py:312
  176.3 1.1 constant_dynamic-slice_fusion.3.res_ref
  177.4 24.1 %all-to-all-done.2 = bf16[4,64,2048]{2,1,0:T(8,128)(2,1)S(1)} async-done(((bf16[4,64,2048]{2,1,0:T(8,128)(2,1)}), bf16[4,64,2048]{2,1,0:T(8,128)(2,1)S(1)}, u32[]{:S(2)}, u32[]{:S(2)}) %all-to-all-start.2) | async-done | bytes 1048608 | tf_op jit(solution)/shard_map/all_to_all | solution.py:312
  201.5 0.4 convolution_convert_fusion.1.att_ref
  201.9 0.0 copy-start.2
  201.9 3.4 %copy-done.2 = bf16[2048,2048]{1,0:T(8,128)(2,1)S(1)} copy-done((bf16[2048,2048]{1,0:T(8,128)(2,1)S(1)}, bf16[2048,2048]{1,0:T(8,128)(2,1)}, u32[]{:S(2)}) %copy-start.2) | copy-done | bytes 8388632
  205.2 55.9 %shard_map.91 = bf16[128,2048]{1,0:T(8,128)(2,1)S(1)} custom-call(bf16[128,2048]{1,0:T(8,128)(2,1)S(1)} %convolution_convert_fusion.1.att_ref, bf16[2048,2048]{1,0:T(8,128)(2,1)S(1)} %copy-done.2, bf16[128,2048]{1,0:T(8,128)(2,1)S(1)} %constant_dynamic-slice_fusion.3.res_ref), custom_call_target="tpu_custom_call" | custom-call | tf_op jit(solution)/shard_map/pallas_call | solution.py:202
  261.2 0.8 copy.68
  261.9 0.0 copy-done.1
  (4 shorter events, 0.0 us)
Async XLA Ops:
  6.5 59.3 %copy-start = (f32[128]{0:T(128)S(1)}, f32[128]{0:T(128)}, u32[]{:S(2)}) copy-start(f32[128]{0:T(128)} %param.11) | copy-start | bytes 1540
  6.5 48.7 %all-gather.2.cloned.1.call-start = ((), (), s32[]{:S(2)}) async-start(), calls=%async_computation.4 | async-start | bytes 3145728 | tf_op jit(solution)/shard_map/all_gather | solution.py:256
  45.4 64.9 %reduce-scatter.2.cloned.1.call-start = ((), (), s32[]{:S(2)}) async-start(), calls=%async_computation.5 | async-start | bytes 2621440 | tf_op jit(solution)/shard_map/reduce_scatter | solution.py:263
  55.2 9.9 %copy-start.3 = (s32[4]{0:T(128)S(1)}, s32[4]{0:T(128)}, u32[]{:S(2)}) copy-start(s32[4]{0:T(128)} %param.17) | copy-start | bytes 52
  55.2 9.9 %copy-start.4 = (s32[128]{0:T(128)S(1)}, s32[128]{0:T(128)}, u32[]{:S(2)}) copy-start(s32[128]{0:T(128)} %param.15) | copy-start | bytes 1540
  55.2 10.1 %copy-start.5 = (s32[128]{0:T(128)S(1)}, s32[128]{0:T(128)}, u32[]{:S(2)}) copy-start(s32[128]{0:T(128)} %param.16) | copy-start | bytes 1540
  115.2 29.3 %all-to-all-start.1 = ((bf16[4,64,2048]{2,1,0:T(8,128)(2,1)}), bf16[4,64,2048]{2,1,0:T(8,128)(2,1)S(1)}, u32[]{:S(2)}, u32[]{:S(2)}) async-start(bf16[4,64,2048]{2,1,0:T(8,128)(2,1)} %bitcast.10), calls=%async_computation.2 | async-start | bytes 2097152 | tf_op jit(solution)/shard_map/all_to_all | solution.py:297
  171.4 90.5 %copy-start.1 = (f32[128]{0:T(128)S(1)}, f32[128]{0:T(128)}, u32[]{:S(2)}) copy-start(f32[128]{0:T(128)} %param.11) | copy-start | bytes 1540
  172.8 28.7 %all-to-all-start.2 = ((bf16[4,64,2048]{2,1,0:T(8,128)(2,1)}), bf16[4,64,2048]{2,1,0:T(8,128)(2,1)S(1)}, u32[]{:S(2)}, u32[]{:S(2)}) async-start(bf16[4,64,2048]{2,1,0:T(8,128)(2,1)} %reshape.61), calls=%async_computation.3 | async-start | bytes 2097152 | tf_op jit(solution)/shard_map/all_to_all | solution.py:312
  201.9 3.4 %copy-start.2 = (bf16[2048,2048]{1,0:T(8,128)(2,1)S(1)}, bf16[2048,2048]{1,0:T(8,128)(2,1)}, u32[]{:S(2)}) copy-start(bf16[2048,2048]{1,0:T(8,128)(2,1)} %w_hbm.1) | copy-start | bytes 25165828
Sparse Core Ops, SparseCore 0:
  45.5 9.6 all-gather.1
  65.2 45.0 reduce-scatter.1
